TPU v7x, 32 devices: a whole 2x2x4 slice. The times are simulated.
32 devices in a mesh: mp: 2 (over core), heads: 8 (over z, y), tok: 2 (over x).
Axes of the slice: x: 2, y: 2, z: 4, core: 2. Of those that a mesh axis runs over, the one named last changes fastest.
Arguments:
- context: bfloat16 [2, 512, 8192], P('mp', None, 'heads'), may hold values from -6 to 6
- out_weight: bfloat16 [2, 8192, 8192], P('mp', 'heads', 'tok'), may hold values from -0.0625 to 0.0625
- skip_states: bfloat16 [2, 512, 8192], P(None, None, 'tok'), may hold values from -6 to 6
- gram_old: float32 [8192, 8192], P('tok', ('mp', 'heads')), may hold values from -1 to 3
- cross_old: float32 [8192, 8192], P('tok', ('mp', 'heads')), may hold values from -30 to 30
- map_old: float32 [8192, 8192], P('tok', ('mp', 'heads')), may hold values from -0.3 to 0.3
Outputs:
- gram_new: float32 [8192, 8192], P('tok', ('mp', 'heads'))
- cross_new: float32 [8192, 8192], P('tok', ('mp', 'heads'))
- map_new: float32 [8192, 8192], P('tok', ('mp', 'heads'))
- residual_new: float32 [8192, 8192], P('tok', ('mp', 'heads'))
All inputs are finite; a program needn't handle non-finite values.
Results may differ from a plain program's by a relative error of at most 0.03.
Values may be sent and summed in bfloat16 or wider, within the bound.
A program may use at most 256 MiB of HBM per device.

v0:
```python
import jax
import jax.numpy as jnp
from jax import lax
from jax.sharding import PartitionSpec as P

decay_keep = 0.75
ridge_weight = 0.1
f32, bf16 = (jnp.float32, jnp.bfloat16)
CHUNKS = 4


def dot(a, b):
    return jnp.dot(a, b, preferred_element_type=f32)


def token_inner(left, right):
    return lax.dot_general(left, right, (((0,), (0,)), ((), ())), preferred_element_type=f32)


def shifted(block, axis, shift):
    n = lax.axis_size(axis)
    return lax.ppermute(block, axis, [(i, (i + shift) % n) for i in range(n)])


def total_over(value, axis):
    n = lax.axis_size(axis)
    if n & n - 1:
        return lax.psum(value, axis)
    bit = 1
    while bit < n:
        value = value + lax.ppermute(value, axis, [(i, i ^ bit) for i in range(n)])
        bit *= 2
    return value


def sum_tok(value):
    n = lax.axis_size("tok")
    half = value.astype(bf16)
    for shift in range(1, n):
        value = value + shifted(half, "tok", shift).astype(f32)
    return value.astype(bf16)


def make_states(context, out_weight, skip_states, width):
    n_tok, n_heads, n_mp = (lax.axis_size(a) for a in ("tok", "heads", "mp"))
    t, h, k = (lax.axis_index(a) for a in ("tok", "heads", "mp"))
    tokens, features = skip_states.shape[1:]
    share = features // n_heads
    part = dot(context[0], out_weight[0]).astype(bf16)
    mine = lax.psum_scatter(part, "heads", scatter_dimension=1, tiled=True)
    skip = lax.dynamic_slice(skip_states, (k, 0, h * share), (1, tokens, share))[0]
    mine = (mine.astype(f32) + skip.astype(f32)).astype(bf16)
    other = lax.ppermute(mine, "mp", [(0, 1), (1, 0)])
    pair = jnp.stack([jnp.where(k == 0, mine, other), jnp.where(k == 0, other, mine)])
    if share == width and n_tok == n_mp == 2:
        away = lax.ppermute(pair, ("mp", "tok"), [(0, 1), (3, 2)])
        columns = jnp.where(k == t, pair, away)
        half = lax.dynamic_slice_in_dim(pair[0], k * (tokens // 2), tokens // 2, 0)
        rows = lax.all_gather(half, "heads", axis=1, tiled=True)
        rows_other = lax.ppermute(rows, "mp", [(0, 1), (1, 0)])
        first = jnp.where(k == 0, rows, rows_other)
        second = jnp.where(k == 0, rows_other, rows)
        source = jnp.concatenate([first, second], 0)
        return (source, columns[0], columns[1])
    both = lax.all_gather(pair, "heads", axis=2, tiled=True)
    whole = lax.all_gather(both, "tok", axis=2, tiled=True)
    columns = lax.dynamic_slice_in_dim(whole, (k * n_heads + h) * width, width, 2)
    return (both[0], columns[0], columns[1])


def per_device(context, out_weight, skip_states, gram_old, cross_old, map_old):
    n_tok = lax.axis_size("tok")
    t = lax.axis_index("tok")
    tokens = context.shape[1]
    height, width = gram_old.shape
    new_weight = (1.0 - decay_keep) / tokens
    step = height // CHUNKS
    cuts = [slice(c * step, (c + 1) * step) for c in range(CHUNKS)]
    map_half = map_old.astype(bf16)
    gram_old_half = gram_old.astype(bf16)
    panels = [
        lax.all_gather(gram_old_half[cut], ("mp", "heads"), axis=1, tiled=True) for cut in cuts
    ]
    maps = [map_half] + [shifted(map_half, "tok", s) for s in range(1, n_tok)]
    source, source_cols, target_cols = make_states(context, out_weight, skip_states, width)
    gram_new = decay_keep * gram_old + new_weight * token_inner(source, source_cols)
    cross_new = decay_keep * cross_old + new_weight * token_inner(source, target_cols)

    def panel_part(panel, s):
        owner = lax.rem(t - s + n_tok, n_tok)
        return lax.dynamic_slice_in_dim(panel, owner * height, height, 1)

    inner_map = sum_tok(dot(source, map_half))
    residuals, halves = ([], [])
    for cut, panel in zip(cuts, panels):
        product = sum((dot(panel_part(panel, s), maps[s]) for s in range(n_tok)))
        low_rank = token_inner(source[:, cut], inner_map)
        residual = (
            cross_new[cut]
            - decay_keep * product
            - new_weight * low_rank
            - ridge_weight * map_old[cut]
        )
        residuals.append(residual)
        halves.append(residual.astype(bf16))
    away = [[shifted(half, "tok", s) for half in halves] for s in range(1, n_tok)]
    inner_residual = sum_tok(sum((dot(source[:, cut], half) for cut, half in zip(cuts, halves))))
    blocks = [jnp.concatenate(halves, 0)] + [jnp.concatenate(a, 0) for a in away]
    applied, squares, mixed = ([], 0.0, 0.0)
    for cut, panel, residual in zip(cuts, panels, residuals):
        product = sum((dot(panel_part(panel, s), blocks[s]) for s in range(n_tok)))
        low_rank = token_inner(source[:, cut], inner_residual)
        value = decay_keep * product + new_weight * low_rank + ridge_weight * residual
        applied.append(value)
        squares = squares + jnp.sum(residual * residual)
        mixed = mixed + jnp.sum(residual * value)
    totals = jnp.stack([squares, mixed])
    for axis in ("mp", "tok", "heads"):
        totals = total_over(totals, axis)
    step_size = totals[0] / totals[1]
    residual = jnp.concatenate(residuals, 0)
    return (
        gram_new,
        cross_new,
        map_old + step_size * residual,
        residual - step_size * jnp.concatenate(applied, 0),
    )


def solution(mesh):
    block = P("tok", ("mp", "heads"))
    placed = (
        P("mp", None, "heads"),
        P("mp", "heads", "tok"),
        P(None, None, "tok"),
        block,
        block,
        block,
    )
    return jax.shard_map(
        per_device, mesh=mesh, in_specs=placed, out_specs=(block,) * 4, check_vma=False
    )
```

profile of v0, /device:TPU:0, one launch (start us, length us, event | category | flops | bytes accessed | tf_op | source)
XLA Modules:
  0.0 842.1 jit_solution(6807376808990272788)
XLA Ops:
  8.4 9.4 %fusion.35 = bf16[512,4096]{1,0:T(8,128)(2,1)} fusion(bf16[1,1024,4096]{2,1,0:T(8,128)(2,1)} %param.7, bf16[1,512,1024]{2,1,0:T(8,128)(2,1)S(1)} %copy-done), kind=kOutput, calls=%fused_computation.49 | convolution fusion | flops 4297064448 | bytes 13631488 | tf_op jit(solution)/shard_map/dot_general | solution.py:13
  17.9 91.3 %reduce-scatter.2.cloned.1.call-done = bf16[512,512]{1,0:T(8,128)(2,1)} async-done(((bf16[512,4096]{1,0:T(8,128)(2,1)}), bf16[512,512]{1,0:T(8,128)(2,1)}) %reduce-scatter.2.cloned.1.call-update) | async-done | bytes 524304 | tf_op jit(solution)/shard_map/reduce_scatter | solution.py:50
  113.3 3.9 convert_element_type.56
  121.1 43.2 %all-gather.6.cloned.1.call-done = bf16[256,4096]{1,0:T(8,128)(2,1)} async-done(((bf16[256,512]{1,0:T(8,128)(2,1)}), bf16[256,4096]{1,0:T(8,128)(2,1)}) %all-gather.6.cloned.1.call-update) | async-done | bytes 2097168 | tf_op jit(solution)/shard_map/all_gather | solution.py:59
  164.4 3.4 collective-permute-start.2
  167.8 6.0 convert_element_type.57
  173.8 11.4 %collective-permute-done.2 = bf16[2,512,512]{2,1,0:T(8,128)(2,1)S(1)} collective-permute-done((bf16[2,512,512]{2,1,0:T(8,128)(2,1)S(1)}, bf16[2,512,512]{2,1,0:T(8,128)(2,1)S(1)}, u32[]{:S(2)}, u32[]{:S(2)}) %collective-permute-start.2) | collective-permute-done | bytes 1048608 | tf_op jit(solution)/shard_map/ppermute | solution.py:56
  185.3 2.6 broadcast_select_fusion.1
  188.0 5.4 fusion.79
  193.4 2.6 collective-permute-start.4
  196.0 5.0 multiply_add_fusion.2
  201.0 4.9 multiply_add_fusion.1
  207.7 73.5 %collective-permute-done.4 = bf16[512,512]{1,0:T(8,128)(2,1)S(1)} collective-permute-done((bf16[512,512]{1,0:T(8,128)(2,1)S(1)}, bf16[512,512]{1,0:T(8,128)(2,1)S(1)}, u32[]{:S(2)}, u32[]{:S(2)}) %collective-permute-start.4) | collective-permute-done | bytes 524320 | tf_op jit(solution)/shard_map/ppermute | solution.py:22
  281.4 14.3 %all-gather.10.cloned.1.call-done = bf16[1024,8192]{1,0:T(8,128)(2,1)} async-done(((bf16[1024,512]{1,0:T(8,128)(2,1)}), bf16[1024,8192]{1,0:T(8,128)(2,1)}) %all-gather.10.cloned.1.call-update) | async-done | bytes 16777232 | tf_op jit(solution)/shard_map/all_gather | solution.py:82
  295.7 8.3 fusion.25
  305.9 6.6 fusion.21
  312.5 5.0 fusion.82
  318.9 107.4 %all-gather.12.cloned.1.call-done = bf16[1024,8192]{1,0:T(8,128)(2,1)} async-done(((bf16[1024,512]{1,0:T(8,128)(2,1)}), bf16[1024,8192]{1,0:T(8,128)(2,1)}) %all-gather.12.cloned.1.call-update) | async-done | bytes 16777232 | tf_op jit(solution)/shard_map/all_gather | solution.py:82
  426.4 8.3 fusion.13
  436.6 6.7 fusion.17
  443.3 5.0 fusion.81
  449.7 107.4 %all-gather.14.cloned.1.call-done = bf16[1024,8192]{1,0:T(8,128)(2,1)} async-done(((bf16[1024,512]{1,0:T(8,128)(2,1)}), bf16[1024,8192]{1,0:T(8,128)(2,1)}) %all-gather.14.cloned.1.call-update) | async-done | bytes 16777232 | tf_op jit(solution)/shard_map/all_gather | solution.py:82
  557.1 8.5 %fusion.5 = f32[1024,512]{1,0:T(8,128)S(1)} fusion(bf16[4096,512]{1,0:T(8,128)(2,1)} %collective-permute-done.3, bf16[1024,8192]{1,0:T(8,128)(2,1)} %all-gather.14.cloned.1.call-done, s32[]{:T(128)S(6)} %select_n.73), kind=kOutput, calls=%fused_computation.10 | convolution fusion | flops 4294967296 | bytes 14680068 | tf_op jit(solution)/shard_map/dot_general | solution.py:13
  567.2 6.7 fusion.9
  574.0 5.3 fusion.80
  580.7 2.9 fusion.85
  583.6 2.9 fusion.86
  586.6 2.9 fusion.87
  589.5 98.3 %all-gather.8.cloned.1.call-done = bf16[1024,8192]{1,0:T(8,128)(2,1)} async-done(((bf16[1024,512]{1,0:T(8,128)(2,1)}), bf16[1024,8192]{1,0:T(8,128)(2,1)}) %all-gather.8.cloned.1.call-update) | async-done | bytes 16777232 | tf_op jit(solution)/shard_map/all_gather | solution.py:82
  687.8 8.3 fusion.29
  697.2 6.6 fusion.33
  703.9 3.6 fusion.83
  710.3 9.2 %fusion.31 = f32[1024,512]{1,0:T(8,128)S(1)} fusion(bf16[1024,8192]{1,0:T(8,128)(2,1)} %all-gather.8.cloned.1.call-done, s32[]{:T(128)S(6)} %select_n.72, bf16[1024,512]{1,0:T(8,128)(2,1)} %get-tuple-element.29, bf16[1024,512]{1,0:T(8,128)(2,1)} %get-tuple-element.31, bf16[1024,512]{1,0:T(8,128)(2,1)} %get-tuple-element.33, ...), kind=kOutput, calls=%fused_computation.36 | convolution fusion | flops 4311744512 | bytes 14680068 | tf_op jit(solution)/shard_map/dot_general | solution.py:13
  719.6 8.8 %fusion.23 = f32[1024,512]{1,0:T(8,128)S(1)} fusion(bf16[1024,8192]{1,0:T(8,128)(2,1)} %all-gather.10.cloned.1.call-done, s32[]{:T(128)S(6)} %select_n.72, bf16[1024,512]{1,0:T(8,128)(2,1)} %get-tuple-element.29, bf16[1024,512]{1,0:T(8,128)(2,1)} %get-tuple-element.31, bf16[1024,512]{1,0:T(8,128)(2,1)} %get-tuple-element.33, ...), kind=kOutput, calls=%fused_computation.28 | convolution fusion | flops 4311744512 | bytes 14680068 | tf_op jit(solution)/shard_map/dot_general | solution.py:13
  728.4 10.0 %fusion.15 = f32[1024,512]{1,0:T(8,128)} fusion(bf16[1024,8192]{1,0:T(8,128)(2,1)} %all-gather.12.cloned.1.call-done, s32[]{:T(128)S(6)} %select_n.72, bf16[1024,512]{1,0:T(8,128)(2,1)} %get-tuple-element.29, bf16[1024,512]{1,0:T(8,128)(2,1)} %get-tuple-element.31, bf16[1024,512]{1,0:T(8,128)(2,1)} %get-tuple-element.33, ...), kind=kOutput, calls=%fused_computation.20 | convolution fusion | flops 4311744512 | bytes 14680068 | tf_op jit(solution)/shard_map/dot_general | solution.py:13
  738.4 10.1 %fusion.7 = f32[1024,512]{1,0:T(8,128)} fusion(bf16[1024,8192]{1,0:T(8,128)(2,1)} %all-gather.14.cloned.1.call-done, s32[]{:T(128)S(6)} %select_n.72, bf16[1024,512]{1,0:T(8,128)(2,1)} %get-tuple-element.29, bf16[1024,512]{1,0:T(8,128)(2,1)} %get-tuple-element.31, bf16[1024,512]{1,0:T(8,128)(2,1)} %get-tuple-element.33, ...), kind=kOutput, calls=%fused_computation.12 | convolution fusion | flops 4311744512 | bytes 14680068 | tf_op jit(solution)/shard_map/dot_general | solution.py:13
  752.7 8.6 %fusion.27 = f32[1024,512]{1,0:T(8,128)S(1)} fusion(bf16[4096,512]{1,0:T(8,128)(2,1)S(1)} %constant_dynamic-update-slice_fusion, bf16[1024,8192]{1,0:T(8,128)(2,1)} %all-gather.8.cloned.1.call-done, s32[]{:T(128)S(6)} %select_n.73), kind=kOutput, calls=%fused_computation.32 | convolution fusion | flops 4294967296 | bytes 14680068 | tf_op jit(solution)/shard_map/dot_general | solution.py:13
  761.4 3.0 multiply_reduce_fusion.7
  764.4 7.1 fusion.19
  771.5 3.2 multiply_reduce_fusion.6
  776.0 8.3 fusion.11
  784.3 3.0 multiply_reduce_fusion.5
  788.0 8.3 fusion.3
  796.3 3.1 multiply_reduce_fusion.4
  808.9 2.1 collective-permute-done.12
  811.0 3.5 collective-permute-done.13
  816.1 2.9 collective-permute-done.14
  820.9 14.1 %fusion = (f32[4096,512]{1,0:T(8,128)}, f32[4096,512]{1,0:T(8,128)}) fusion(f32[1024,512]{1,0:T(8,128)} %get-tuple-element.42, f32[1024,512]{1,0:T(8,128)} %get-tuple-element.41, f32[1024,512]{1,0:T(8,128)} %get-tuple-element.40, f32[1024,512]{1,0:T(8,128)} %get-tuple-element.39, f32[1024,512]{1,0:T(8,128)} %get-tuple-element.30, ...), kind=kLoop, calls=%fused_computation.2 | loop fusion | flops 20971520 | bytes 41943044 | tf_op jit(solution)/shard_map/sub | solution.py:126
  (118 shorter events, 37.9 us)
Async XLA Ops:
  7.2 102.0 %reduce-scatter.2.cloned.1.call-start = ((), (), s32[]{:S(2)}) async-start(), calls=%async_computation.1 | async-start | bytes 4718592 | tf_op jit(solution)/shard_map/reduce_scatter | solution.py:50
  17.8 146.5 %all-gather.6.cloned.1.call-start = ((), (), s32[]{:S(2)}) async-start(), calls=%async_computation.2 | async-start | bytes 2359296 | tf_op jit(solution)/shard_map/all_gather | solution.py:59
  110.5 2.0 collective-permute-start
  113.3 182.4 %all-gather.10.cloned.1.call-start = ((), (), s32[]{:S(2)}) async-start(), calls=%async_computation.4 | async-start | bytes 17825792 | tf_op jit(solution)/shard_map/all_gather | solution.py:82
  119.4 307.0 %all-gather.12.cloned.1.call-start = ((), (), s32[]{:S(2)}) async-start(), calls=%async_computation.5 | async-start | bytes 17825792 | tf_op jit(solution)/shard_map/all_gather | solution.py:82
  119.9 437.1 %all-gather.14.cloned.1.call-start = ((), (), s32[]{:S(2)}) async-start(), calls=%async_computation.6 | async-start | bytes 17825792 | tf_op jit(solution)/shard_map/all_gather | solution.py:82
  120.5 567.2 %all-gather.8.cloned.1.call-start = ((), (), s32[]{:S(2)}) async-start(), calls=%async_computation.3 | async-start | bytes 17825792 | tf_op jit(solution)/shard_map/all_gather | solution.py:82
  164.3 21.0 %collective-permute-start.1 = (bf16[256,4096]{1,0:T(8,128)(2,1)}, bf16[256,4096]{1,0:T(8,128)(2,1)}, u32[]{:S(2)}, u32[]{:S(2)}) collective-permute-start(bf16[256,4096]{1,0:T(8,128)(2,1)} %all-gather.6.cloned.1.call-done), channel_id=1, source_target_pairs={{0,16},{16,0},{1,17},{17,1},{2,18},{18,2},{3,19},{19,3},{4,20},{20... | collective-permute-start | bytes 6291464 | tf_op jit(solution)/shard_map/ppermute | solution.py:60
  164.4 20.8 %collective-permute-start.2 = (bf16[2,512,512]{2,1,0:T(8,128)(2,1)S(1)}, bf16[2,512,512]{2,1,0:T(8,128)(2,1)S(1)}, u32[]{:S(2)}, u32[]{:S(2)}) collective-permute-start(bf16[2,512,512]{2,1,0:T(8,128)(2,1)S(1)} %pad_maximum_fusion.6), channel_id=1, source_target_pairs={{0,1},{17,16},{2,3},{19,18},{4,5},{21,20},{6,7},{23,22},{8,9},{25,... | collective-permute-start | bytes 3145736 | tf_op jit(solution)/shard_map/ppermute | solution.py:56
  173.8 130.2 %collective-permute-start.3 = (bf16[4096,512]{1,0:T(8,128)(2,1)}, bf16[4096,512]{1,0:T(8,128)(2,1)}, u32[]{:S(2)}, u32[]{:S(2)}) collective-permute-start(bf16[4096,512]{1,0:T(8,128)(2,1)} %convert_element_type.57), channel_id=1, source_target_pairs={{0,1},{1,0},{2,3},{3,2},{4,5},{5,4},{6,7},{7,6},{8,9},{9,8},{10,11... | collective-permute-start | bytes 12582920 | tf_op jit(solution)/shard_map/ppermute | solution.py:22
  185.3 10.7 %slice-start = ((s8[8388608]{0:T(1024)(128)(4,1)}), s8[4194304]{0:T(1024)(128)(4,1)S(1)}, s32[]{:S(2)}) async-start(s8[8388608]{0:T(1024)(128)(4,1)} %bitcast.57), calls=%async_computation.7 | async-start | bytes 8388608
  188.0 17.9 %copy-start.2 = (bf16[256,4096]{1,0:T(8,128)(2,1)}, bf16[256,4096]{1,0:T(8,128)(2,1)S(1)}, u32[]{:S(2)}) copy-start(bf16[256,4096]{1,0:T(8,128)(2,1)S(1)} %get-tuple-element.22) | copy-start | bytes 6291460
  188.0 8.0 slice-start.1
  193.4 7.6 slice-start.2
  193.4 7.6 slice-start.3
  193.4 87.8 %collective-permute-start.4 = (bf16[512,512]{1,0:T(8,128)(2,1)S(1)}, bf16[512,512]{1,0:T(8,128)(2,1)S(1)}, u32[]{:S(2)}, u32[]{:S(2)}) collective-permute-start(bf16[512,512]{1,0:T(8,128)(2,1)S(1)} %get-tuple-element.27), channel_id=1, source_target_pairs={{0,1},{1,0},{2,3},{3,2},{4,5},{5,4},{6,7},{7,6},{8,9},{9,8},{10,11... | collective-permute-start | bytes 1572872 | tf_op jit(solution)/shard_map/ppermute | solution.py:22
  295.7 10.2 %copy-start.24 = (bf16[1024,8192]{1,0:T(8,128)(2,1)S(1)}, bf16[1024,8192]{1,0:T(8,128)(2,1)}, u32[]{:S(2)}) copy-start(bf16[1024,8192]{1,0:T(8,128)(2,1)} %all-gather.10.cloned.1.call-done) | copy-start | bytes 50331652
  304.0 8.5 %copy-start.13 = (bf16[512,1024]{1,0:T(8,128)(2,1)S(1)}, bf16[512,1024]{1,0:T(8,128)(2,1)}, u32[]{:S(2)}) copy-start(bf16[512,1024]{1,0:T(8,128)(2,1)} %get-tuple-element.18) | copy-start | bytes 3145732
  317.5 431.3 %collective-permute-start.6 = (bf16[1024,512]{1,0:T(8,128)(2,1)}, bf16[1024,512]{1,0:T(8,128)(2,1)}, u32[]{:S(2)}, u32[]{:S(2)}) collective-permute-start(bf16[1024,512]{1,0:T(8,128)(2,1)} %get-tuple-element.33), channel_id=1, source_target_pairs={{0,1},{1,0},{2,3},{3,2},{4,5},{5,4},{6,7},{7,6},{8,9},{9,8},{10,11... | collective-permute-start | bytes 3145736 | tf_op jit(solution)/shard_map/ppermute | solution.py:22
  426.4 10.2 %copy-start.23 = (bf16[1024,8192]{1,0:T(8,128)(2,1)S(1)}, bf16[1024,8192]{1,0:T(8,128)(2,1)}, u32[]{:S(2)}) copy-start(bf16[1024,8192]{1,0:T(8,128)(2,1)} %all-gather.12.cloned.1.call-done) | copy-start | bytes 50331652
  436.6 6.7 copy-start.10
  448.3 301.8 %collective-permute-start.7 = (bf16[1024,512]{1,0:T(8,128)(2,1)}, bf16[1024,512]{1,0:T(8,128)(2,1)}, u32[]{:S(2)}, u32[]{:S(2)}) collective-permute-start(bf16[1024,512]{1,0:T(8,128)(2,1)} %get-tuple-element.31), channel_id=1, source_target_pairs={{0,1},{1,0},{2,3},{3,2},{4,5},{5,4},{6,7},{7,6},{8,9},{9,8},{10,11... | collective-permute-start | bytes 3145736 | tf_op jit(solution)/shard_map/ppermute | solution.py:22
  557.1 10.2 %copy-start.22 = (bf16[1024,8192]{1,0:T(8,128)(2,1)S(1)}, bf16[1024,8192]{1,0:T(8,128)(2,1)}, u32[]{:S(2)}) copy-start(bf16[1024,8192]{1,0:T(8,128)(2,1)} %all-gather.14.cloned.1.call-done) | copy-start | bytes 50331652
  567.2 6.7 copy-start.8
  574.0 6.7 copy-start.14
  574.0 9.7 %copy-start.11 = (bf16[512,1024]{1,0:T(8,128)(2,1)S(1)}, bf16[512,1024]{1,0:T(8,128)(2,1)}, u32[]{:S(2)}) copy-start(bf16[512,1024]{1,0:T(8,128)(2,1)} %get-tuple-element.19) | copy-start | bytes 3145732
  579.3 172.2 %collective-permute-start.8 = (bf16[1024,512]{1,0:T(8,128)(2,1)}, bf16[1024,512]{1,0:T(8,128)(2,1)}, u32[]{:S(2)}, u32[]{:S(2)}) collective-permute-start(bf16[1024,512]{1,0:T(8,128)(2,1)} %get-tuple-element.29), channel_id=1, source_target_pairs={{0,1},{1,0},{2,3},{3,2},{4,5},{5,4},{6,7},{7,6},{8,9},{9,8},{10,11... | collective-permute-start | bytes 3145736 | tf_op jit(solution)/shard_map/ppermute | solution.py:22
  687.8 9.4 %copy-start.25 = (bf16[1024,8192]{1,0:T(8,128)(2,1)S(1)}, bf16[1024,8192]{1,0:T(8,128)(2,1)}, u32[]{:S(2)}) copy-start(bf16[1024,8192]{1,0:T(8,128)(2,1)} %all-gather.8.cloned.1.call-done) | copy-start | bytes 50331652
  697.2 6.7 copy-start.3
  703.8 5.1 copy-start.18
  707.4 53.9 %copy-start.7 = (f32[1024,512]{1,0:T(8,128)}, f32[1024,512]{1,0:T(8,128)S(1)}, u32[]{:S(2)}) copy-start(f32[1024,512]{1,0:T(8,128)S(1)} %get-tuple-element.36) | copy-start | bytes 6291460
  707.4 41.3 %collective-permute-start.5 = (bf16[1024,512]{1,0:T(8,128)(2,1)S(1)}, bf16[1024,512]{1,0:T(8,128)(2,1)S(1)}, u32[]{:S(2)}, u32[]{:S(2)}) collective-permute-start(bf16[1024,512]{1,0:T(8,128)(2,1)S(1)} %get-tuple-element.35), channel_id=1, source_target_pairs={{0,1},{1,0},{2,3},{3,2},{4,5},{5,4},{6,7},{7,6},{8,9},{9,8},{10,11... | collective-permute-start | bytes 3145736 | tf_op jit(solution)/shard_map/ppermute | solution.py:22
  709.7 38.8 %collective-permute-start.9 = (bf16[512,512]{1,0:T(8,128)(2,1)S(1)}, bf16[512,512]{1,0:T(8,128)(2,1)S(1)}, u32[]{:S(2)}, u32[]{:S(2)}) collective-permute-start(bf16[512,512]{1,0:T(8,128)(2,1)S(1)} %get-tuple-element.37), channel_id=1, source_target_pairs={{0,1},{1,0},{2,3},{3,2},{4,5},{5,4},{6,7},{7,6},{8,9},{9,8},{10,11... | collective-permute-start | bytes 1572872 | tf_op jit(solution)/shard_map/ppermute | solution.py:22
  752.7 11.7 %copy-start.21 = (bf16[4096,512]{1,0:T(8,128)(2,1)}, bf16[4096,512]{1,0:T(8,128)(2,1)S(1)}, u32[]{:S(2)}) copy-start(bf16[4096,512]{1,0:T(8,128)(2,1)S(1)} %constant_dynamic-update-slice_fusion) | copy-start | bytes 12582916
  764.4 7.1 copy-start.4
  764.4 7.1 copy-start.15
  775.9 8.3 copy-start.5
  775.9 8.3 copy-start.12
  776.0 8.3 copy-start.17
  788.0 8.3 copy-start.6
  788.0 8.3 copy-start.9
  788.0 8.3 copy-start.16
  802.6 1.1 collective-permute-start.10
  803.9 3.5 collective-permute-start.11
  807.5 3.5 collective-permute-start.12
  811.0 3.5 collective-permute-start.13
  814.6 4.4 collective-permute-start.14
  820.9 14.1 %copy-start.1 = (bf16[1,512,1024]{2,1,0:T(8,128)(2,1)S(1)}, bf16[1,512,1024]{2,1,0:T(8,128)(2,1)}, u32[]{:S(2)}) copy-start(bf16[1,512,1024]{2,1,0:T(8,128)(2,1)} %param.6) | copy-start | bytes 3145732
  (3 other events, 11.5 us)
Sparse Core Ops, SparseCore 0:
  17.9 91.1 reduce-scatter.1
  113.4 50.8 all-gather.5
  167.1 128.5 all-gather.9
  297.8 128.5 all-gather.11
  428.5 128.5 all-gather.13
  559.2 128.5 all-gather.7
where the time goes:
time: 848 us; the launch traced here: 842 us
  waiting for transfers between devices  562 us (66%)
  matrix products  196 us (23%)
  other arithmetic  30.7 us (4%)
  between operations  21.2 us (2%)
  starting transfers between devices  17.1 us (2%)
  local copies, waits for them, and re-layouts  15.3 us (2%)
    all_gather x4, waiting for transfers between devices, per_device(): lax.all_gather(gram_old_half[cut], ('mp', 'heads'), axis=1, tiled=True)  327 us
    dot_general x22, matrix products, dot(): return jnp.dot(a, b, preferred_element_type=f32)  155 us
    reduce_scatter x1, waiting for transfers between devices, make_states(): mine = lax.psum_scatter(part, 'heads', scatter_dimension=1, tiled=True)  91.3 us
    ppermute x7, waiting for transfers between devices, shifted(): return lax.ppermute(block, axis, [(i, (i + shift) % n) for i in range(n)])  73.5 us
    all_gather x1, waiting for transfers between devices, make_states(): rows = lax.all_gather(half, 'heads', axis=1, tiled=True)  43.2 us
    dot_general x10, matrix products, token_inner(): lax.dot_general(left, right, (((0,), (0,)), ((), ())), preferred_element_...  41.2 us
  transfers between devices with their start and end apart: 21, of which 14 were waited for; matrix products, arithmetic and copies ran while one was open for 19% of the time, Pallas kernels for 0%

commit v1 on v0

--- a/solution.py
+++ b/solution.py
@@ -56,7 +56,17 @@
         away = lax.ppermute(pair, ("mp", "tok"), [(0, 1), (3, 2)])
         columns = jnp.where(k == t, pair, away)
         half = lax.dynamic_slice_in_dim(pair[0], k * (tokens // 2), tokens // 2, 0)
-        rows = lax.all_gather(half, "heads", axis=1, tiled=True)
+        axis_len = lax.axis_size("heads")
+        f_now = sorted(((k0, (k0 + 1) % axis_len) for k0 in range(axis_len)))
+        k_now = half
+        buffers = [k_now]
+        dev_j = 1
+        while dev_j < axis_len:
+            k_now = lax.ppermute(k_now, "heads", perm=f_now)
+            buffers.insert(0, k_now)
+            dev_j += 1
+        state_next = jnp.concatenate(buffers, axis=1)
+        rows = jnp.roll(state_next, (lax.axis_index("heads") + 1) * half.shape[1], axis=1)
         rows_other = lax.ppermute(rows, "mp", [(0, 1), (1, 0)])
         first = jnp.where(k == 0, rows, rows_other)
         second = jnp.where(k == 0, rows_other, rows)

time: 848 us -> 763 us (0.90)
  waiting for transfers between devices: 562 us -> 468 us
    all_gather x4, waiting for transfers between devices: 327 us -> 100 us  [per_device(): lax.all_gather(gram_old_half[cut], ('mp', 'heads'), axis=1, tiled=True)]
    ppermute x0 -> x7, waiting for transfers between devices: none -> 110 us  [make_states(): k_now = lax.ppermute(k_now, 'heads', perm=f_now)]
    reduce_scatter x1, waiting for transfers between devices: 91.3 us -> 160 us  [make_states(): mine = lax.psum_scatter(part, 'heads', scatter_dimension=1, tiled=True)]
    all_gather x1 -> x0, waiting for transfers between devices: 43.2 us -> none  [make_states(): rows = lax.all_gather(half, 'heads', axis=1, tiled=True)]
  transfers between devices with their start and end apart: 21 -> 27, of which waited for: 14 -> 18; matrix products, arithmetic and copies ran while one was open for 19% -> 22% of each run, Pallas kernels for 0% -> 0%
where the time goes in v1:
time: 763 us; the launch traced here: 756 us
  waiting for transfers between devices  468 us (61%)
  matrix products  196 us (26%)
  other arithmetic  32.6 us (4%)
  between operations  22.8 us (3%)
  starting transfers between devices  21.1 us (3%)
  local copies, waits for them, and re-layouts  15.8 us (2%)
    reduce_scatter x1, waiting for transfers between devices, make_states(): mine = lax.psum_scatter(part, 'heads', scatter_dimension=1, tiled=True)  160 us
    dot_general x22, matrix products, dot(): return jnp.dot(a, b, preferred_element_type=f32)  155 us
    ppermute x7, waiting for transfers between devices, make_states(): k_now = lax.ppermute(k_now, 'heads', perm=f_now)  110 us
    all_gather x4, waiting for transfers between devices, per_device(): lax.all_gather(gram_old_half[cut], ('mp', 'heads'), axis=1, tiled=True)  100 us
    ppermute x7, waiting for transfers between devices, shifted(): return lax.ppermute(block, axis, [(i, (i + shift) % n) for i in range(n)])  72.1 us
    dot_general x10, matrix products, token_inner(): lax.dot_general(left, right, (((0,), (0,)), ((), ())), preferred_element_...  41.3 us
  transfers between devices with their start and end apart: 27, of which 18 were waited for; matrix products, arithmetic and copies ran while one was open for 22% of the time, Pallas kernels for 0%

profile of v1, /device:TPU:0, one launch (start us, length us, event | category | flops | bytes accessed | tf_op | source)
XLA Modules:
  0.0 755.9 jit_solution(13386755793787375833)
XLA Ops:
  9.2 9.4 %fusion.35 = bf16[512,4096]{1,0:T(8,128)(2,1)} fusion(bf16[1,1024,4096]{2,1,0:T(8,128)(2,1)} %param.7, bf16[1,512,1024]{2,1,0:T(8,128)(2,1)S(1)} %copy-done), kind=kOutput, calls=%fused_computation.49 | convolution fusion | flops 4297064448 | bytes 13631488 | tf_op jit(solution)/shard_map/dot_general | solution.py:13
  18.7 3.9 convert_element_type.56
  26.6 160.3 %reduce-scatter.2.cloned.1.call-done = bf16[512,512]{1,0:T(8,128)(2,1)} async-done(((bf16[512,4096]{1,0:T(8,128)(2,1)}), bf16[512,512]{1,0:T(8,128)(2,1)}) %reduce-scatter.2.cloned.1.call-update) | async-done | bytes 524304 | tf_op jit(solution)/shard_map/reduce_scatter | solution.py:50
  191.8 15.0 %collective-permute-done.1 = bf16[256,512]{1,0:T(8,128)(2,1)S(1)} collective-permute-done((bf16[256,512]{1,0:T(8,128)(2,1)S(1)}, bf16[256,512]{1,0:T(8,128)(2,1)S(1)}, u32[]{:S(2)}, u32[]{:S(2)}) %collective-permute-start.1) | collective-permute-done | bytes 262176 | tf_op jit(solution)/shard_map/ppermute | solution.py:65
  206.8 16.9 %collective-permute-done.2 = bf16[256,512]{1,0:T(8,128)(2,1)S(1)} collective-permute-done((bf16[256,512]{1,0:T(8,128)(2,1)S(1)}, bf16[256,512]{1,0:T(8,128)(2,1)S(1)}, u32[]{:S(2)}, u32[]{:S(2)}) %collective-permute-start.2) | collective-permute-done | bytes 262176 | tf_op jit(solution)/shard_map/ppermute | solution.py:65
  223.7 15.4 %collective-permute-done.3 = bf16[256,512]{1,0:T(8,128)(2,1)S(1)} collective-permute-done((bf16[256,512]{1,0:T(8,128)(2,1)S(1)}, bf16[256,512]{1,0:T(8,128)(2,1)S(1)}, u32[]{:S(2)}, u32[]{:S(2)}) %collective-permute-start.3) | collective-permute-done | bytes 262176 | tf_op jit(solution)/shard_map/ppermute | solution.py:65
  239.1 14.2 %collective-permute-done.4 = bf16[256,512]{1,0:T(8,128)(2,1)S(1)} collective-permute-done((bf16[256,512]{1,0:T(8,128)(2,1)S(1)}, bf16[256,512]{1,0:T(8,128)(2,1)S(1)}, u32[]{:S(2)}, u32[]{:S(2)}) %collective-permute-start.4) | collective-permute-done | bytes 262176 | tf_op jit(solution)/shard_map/ppermute | solution.py:65
  253.3 15.7 %collective-permute-done.5 = bf16[256,512]{1,0:T(8,128)(2,1)S(1)} collective-permute-done((bf16[256,512]{1,0:T(8,128)(2,1)S(1)}, bf16[256,512]{1,0:T(8,128)(2,1)S(1)}, u32[]{:S(2)}, u32[]{:S(2)}) %collective-permute-start.5) | collective-permute-done | bytes 262176 | tf_op jit(solution)/shard_map/ppermute | solution.py:65
  269.0 15.7 %collective-permute-done.6 = bf16[256,512]{1,0:T(8,128)(2,1)S(1)} collective-permute-done((bf16[256,512]{1,0:T(8,128)(2,1)S(1)}, bf16[256,512]{1,0:T(8,128)(2,1)S(1)}, u32[]{:S(2)}, u32[]{:S(2)}) %collective-permute-start.6) | collective-permute-done | bytes 262176 | tf_op jit(solution)/shard_map/ppermute | solution.py:65
  284.7 17.6 %collective-permute-done.7 = bf16[256,512]{1,0:T(8,128)(2,1)S(1)} collective-permute-done((bf16[256,512]{1,0:T(8,128)(2,1)S(1)}, bf16[256,512]{1,0:T(8,128)(2,1)S(1)}, u32[]{:S(2)}, u32[]{:S(2)}) %collective-permute-start.7) | collective-permute-done | bytes 262176 | tf_op jit(solution)/shard_map/ppermute | solution.py:65
  306.1 4.5 collective-permute-start.9
  310.6 6.4 convert_element_type.57
  317.1 9.4 %collective-permute-done.9 = bf16[2,512,512]{2,1,0:T(8,128)(2,1)} collective-permute-done((bf16[2,512,512]{2,1,0:T(8,128)(2,1)}, bf16[2,512,512]{2,1,0:T(8,128)(2,1)}, u32[]{:S(2)}, u32[]{:S(2)}) %collective-permute-start.9) | collective-permute-done | bytes 1048608 | tf_op jit(solution)/shard_map/ppermute | solution.py:56
  326.6 3.2 broadcast_select_fusion.1
  329.8 5.3 fusion.79
  335.2 4.4 collective-permute-start.11
  339.6 5.0 multiply_add_fusion.2
  344.6 4.9 multiply_add_fusion.1
  351.2 72.1 %collective-permute-done.11 = bf16[512,512]{1,0:T(8,128)(2,1)S(1)} collective-permute-done((bf16[512,512]{1,0:T(8,128)(2,1)S(1)}, bf16[512,512]{1,0:T(8,128)(2,1)S(1)}, u32[]{:S(2)}, u32[]{:S(2)}) %collective-permute-start.11) | collective-permute-done | bytes 524320 | tf_op jit(solution)/shard_map/ppermute | solution.py:22
  423.5 8.3 %fusion.25 = f32[1024,512]{1,0:T(8,128)S(1)} fusion(bf16[4096,512]{1,0:T(8,128)(2,1)} %convert_element_type.57, bf16[1024,8192]{1,0:T(8,128)(2,1)} %all-gather.7.cloned.1.call-done, s32[]{:T(128)S(6)} %select_n.87), kind=kOutput, calls=%fused_computation.30 | convolution fusion | flops 4294967296 | bytes 14680068 | tf_op jit(solution)/shard_map/dot_general | solution.py:13
  433.0 6.5 fusion.21
  439.5 5.3 fusion.82
  447.2 8.3 %fusion.13 = f32[1024,512]{1,0:T(8,128)S(1)} fusion(bf16[4096,512]{1,0:T(8,128)(2,1)} %collective-permute-done.10, bf16[1024,8192]{1,0:T(8,128)(2,1)} %all-gather.9.cloned.1.call-done, s32[]{:T(128)S(6)} %select_n.88), kind=kOutput, calls=%fused_computation.18 | convolution fusion | flops 4294967296 | bytes 14680068 | tf_op jit(solution)/shard_map/dot_general | solution.py:13
  456.8 6.6 fusion.17
  463.4 5.1 fusion.81
  470.5 8.5 %fusion.5 = f32[1024,512]{1,0:T(8,128)S(1)} fusion(bf16[4096,512]{1,0:T(8,128)(2,1)} %collective-permute-done.10, bf16[1024,8192]{1,0:T(8,128)(2,1)} %all-gather.11.cloned.1.call-done, s32[]{:T(128)S(6)} %select_n.88), kind=kOutput, calls=%fused_computation.10 | convolution fusion | flops 4294967296 | bytes 14680068 | tf_op jit(solution)/shard_map/dot_general | solution.py:13
  480.7 6.7 fusion.9
  487.4 5.3 fusion.80
  497.0 2.9 fusion.86
  499.9 3.0 fusion.87
  502.9 98.0 %all-gather.5.cloned.1.call-done = bf16[1024,8192]{1,0:T(8,128)(2,1)} async-done(((bf16[1024,512]{1,0:T(8,128)(2,1)}), bf16[1024,8192]{1,0:T(8,128)(2,1)}) %all-gather.5.cloned.1.call-update) | async-done | bytes 16777232 | tf_op jit(solution)/shard_map/all_gather | solution.py:92
  601.0 8.3 %fusion.29 = f32[1024,512]{1,0:T(8,128)S(1)} fusion(bf16[4096,512]{1,0:T(8,128)(2,1)} %collective-permute-done.10, bf16[1024,8192]{1,0:T(8,128)(2,1)} %all-gather.5.cloned.1.call-done, s32[]{:T(128)S(6)} %select_n.88), kind=kOutput, calls=%fused_computation.34 | convolution fusion | flops 4294967296 | bytes 14680068 | tf_op jit(solution)/shard_map/dot_general | solution.py:13
  610.4 6.6 fusion.33
  617.1 3.5 fusion.83
  623.5 9.2 %fusion.31 = f32[1024,512]{1,0:T(8,128)S(1)} fusion(bf16[1024,8192]{1,0:T(8,128)(2,1)} %all-gather.5.cloned.1.call-done, s32[]{:T(128)S(6)} %select_n.87, bf16[1024,512]{1,0:T(8,128)(2,1)} %get-tuple-element.29, bf16[1024,512]{1,0:T(8,128)(2,1)} %get-tuple-element.31, bf16[1024,512]{1,0:T(8,128)(2,1)} %get-tuple-element.33, ...), kind=kOutput, calls=%fused_computation.36 | convolution fusion | flops 4311744512 | bytes 14680068 | tf_op jit(solution)/shard_map/dot_general | solution.py:13
  632.8 8.8 %fusion.23 = f32[1024,512]{1,0:T(8,128)S(1)} fusion(bf16[1024,8192]{1,0:T(8,128)(2,1)} %all-gather.7.cloned.1.call-done, s32[]{:T(128)S(6)} %select_n.87, bf16[1024,512]{1,0:T(8,128)(2,1)} %get-tuple-element.29, bf16[1024,512]{1,0:T(8,128)(2,1)} %get-tuple-element.31, bf16[1024,512]{1,0:T(8,128)(2,1)} %get-tuple-element.33, ...), kind=kOutput, calls=%fused_computation.28 | convolution fusion | flops 4311744512 | bytes 14680068 | tf_op jit(solution)/shard_map/dot_general | solution.py:13
  641.6 10.2 %fusion.15 = f32[1024,512]{1,0:T(8,128)} fusion(bf16[1024,8192]{1,0:T(8,128)(2,1)} %all-gather.9.cloned.1.call-done, s32[]{:T(128)S(6)} %select_n.87, bf16[1024,512]{1,0:T(8,128)(2,1)} %get-tuple-element.29, bf16[1024,512]{1,0:T(8,128)(2,1)} %get-tuple-element.31, bf16[1024,512]{1,0:T(8,128)(2,1)} %get-tuple-element.33, ...), kind=kOutput, calls=%fused_computation.20 | convolution fusion | flops 4311744512 | bytes 14680068 | tf_op jit(solution)/shard_map/dot_general | solution.py:13
  651.8 10.0 %fusion.7 = f32[1024,512]{1,0:T(8,128)} fusion(bf16[1024,8192]{1,0:T(8,128)(2,1)} %all-gather.11.cloned.1.call-done, s32[]{:T(128)S(6)} %select_n.87, bf16[1024,512]{1,0:T(8,128)(2,1)} %get-tuple-element.29, bf16[1024,512]{1,0:T(8,128)(2,1)} %get-tuple-element.31, bf16[1024,512]{1,0:T(8,128)(2,1)} %get-tuple-element.33, ...), kind=kOutput, calls=%fused_computation.12 | convolution fusion | flops 4311744512 | bytes 14680068 | tf_op jit(solution)/shard_map/dot_general | solution.py:13
  666.1 8.6 %fusion.27 = f32[1024,512]{1,0:T(8,128)S(1)} fusion(bf16[4096,512]{1,0:T(8,128)(2,1)S(1)} %constant_dynamic-update-slice_fusion.16, bf16[1024,8192]{1,0:T(8,128)(2,1)} %all-gather.5.cloned.1.call-done, s32[]{:T(128)S(6)} %select_n.88), kind=kOutput, calls=%fused_computation.32 | convolution fusion | flops 4294967296 | bytes 14680068 | tf_op jit(solution)/shard_map/dot_general | solution.py:13
  674.7 3.1 multiply_reduce_fusion.7
  677.8 7.1 fusion.19
  684.9 3.0 multiply_reduce_fusion.6
  689.1 8.3 %fusion.11 = f32[1024,512]{1,0:T(8,128)S(1)} fusion(bf16[4096,512]{1,0:T(8,128)(2,1)} %copy-done.22, bf16[1024,8192]{1,0:T(8,128)(2,1)} %all-gather.9.cloned.1.call-done, s32[]{:T(128)S(6)} %select_n.88), kind=kOutput, calls=%fused_computation.16 | convolution fusion | flops 4294967296 | bytes 14680068 | tf_op jit(solution)/shard_map/dot_general | solution.py:13
  697.4 3.1 multiply_reduce_fusion.5
  701.2 8.3 %fusion.3 = f32[1024,512]{1,0:T(8,128)S(1)} fusion(bf16[4096,512]{1,0:T(8,128)(2,1)} %copy-done.22, bf16[1024,8192]{1,0:T(8,128)(2,1)} %all-gather.11.cloned.1.call-done, s32[]{:T(128)S(6)} %select_n.88), kind=kOutput, calls=%fused_computation.8 | convolution fusion | flops 4294967296 | bytes 14680068 | tf_op jit(solution)/shard_map/dot_general | solution.py:13
  709.5 3.1 multiply_reduce_fusion.4
  724.1 3.5 collective-permute-done.20
  734.0 14.1 %fusion = (f32[4096,512]{1,0:T(8,128)}, f32[4096,512]{1,0:T(8,128)}) fusion(f32[1024,512]{1,0:T(8,128)} %get-tuple-element.42, f32[1024,512]{1,0:T(8,128)} %get-tuple-element.41, f32[1024,512]{1,0:T(8,128)} %get-tuple-element.40, f32[1024,512]{1,0:T(8,128)} %get-tuple-element.39, f32[1024,512]{1,0:T(8,128)} %get-tuple-element.30, ...), kind=kLoop, calls=%fused_computation.2 | loop fusion | flops 20971520 | bytes 41943044 | tf_op jit(solution)/shard_map/sub | solution.py:136
  (148 shorter events, 50.6 us)
Async XLA Ops:
  8.0 178.9 %reduce-scatter.2.cloned.1.call-start = ((), (), s32[]{:S(2)}) async-start(), calls=%async_computation.1 | async-start | bytes 4718592 | tf_op jit(solution)/shard_map/reduce_scatter | solution.py:50
  18.6 404.9 %all-gather.7.cloned.1.call-start = ((), (), s32[]{:S(2)}) async-start(), calls=%async_computation.3 | async-start | bytes 17825792 | tf_op jit(solution)/shard_map/all_gather | solution.py:92
  24.7 422.4 %all-gather.9.cloned.1.call-start = ((), (), s32[]{:S(2)}) async-start(), calls=%async_computation.4 | async-start | bytes 17825792 | tf_op jit(solution)/shard_map/all_gather | solution.py:92
  25.3 445.2 %all-gather.11.cloned.1.call-start = ((), (), s32[]{:S(2)}) async-start(), calls=%async_computation.5 | async-start | bytes 17825792 | tf_op jit(solution)/shard_map/all_gather | solution.py:92
  25.9 575.1 %all-gather.5.cloned.1.call-start = ((), (), s32[]{:S(2)}) async-start(), calls=%async_computation.2 | async-start | bytes 17825792 | tf_op jit(solution)/shard_map/all_gather | solution.py:92
  188.2 2.0 collective-permute-start
  190.3 16.5 %collective-permute-start.1 = (bf16[256,512]{1,0:T(8,128)(2,1)S(1)}, bf16[256,512]{1,0:T(8,128)(2,1)S(1)}, u32[]{:S(2)}, u32[]{:S(2)}) collective-permute-start(bf16[256,512]{1,0:T(8,128)(2,1)S(1)} %constant_dynamic-slice_fusion.1), channel_id=1, source_target_pairs={{0,2},{2,4},{4,6},{6,8},{8,10},{10,12},{12,14},{14,0},{1,3},{3,5},... | collective-permute-start | bytes 786440 | tf_op jit(solution)/shard_map/ppermute | solution.py:65
  206.8 16.9 %collective-permute-start.2 = (bf16[256,512]{1,0:T(8,128)(2,1)S(1)}, bf16[256,512]{1,0:T(8,128)(2,1)S(1)}, u32[]{:S(2)}, u32[]{:S(2)}) collective-permute-start(bf16[256,512]{1,0:T(8,128)(2,1)S(1)} %collective-permute-done.1), channel_id=1, source_target_pairs={{0,2},{2,4},{4,6},{6,8},{8,10},{10,12},{12,14},{14,0},{1,3},{3,5},... | collective-permute-start | bytes 786440 | tf_op jit(solution)/shard_map/ppermute | solution.py:65
  223.7 15.4 %collective-permute-start.3 = (bf16[256,512]{1,0:T(8,128)(2,1)S(1)}, bf16[256,512]{1,0:T(8,128)(2,1)S(1)}, u32[]{:S(2)}, u32[]{:S(2)}) collective-permute-start(bf16[256,512]{1,0:T(8,128)(2,1)S(1)} %collective-permute-done.2), channel_id=1, source_target_pairs={{0,2},{2,4},{4,6},{6,8},{8,10},{10,12},{12,14},{14,0},{1,3},{3,5},... | collective-permute-start | bytes 786440 | tf_op jit(solution)/shard_map/ppermute | solution.py:65
  239.1 14.2 %collective-permute-start.4 = (bf16[256,512]{1,0:T(8,128)(2,1)S(1)}, bf16[256,512]{1,0:T(8,128)(2,1)S(1)}, u32[]{:S(2)}, u32[]{:S(2)}) collective-permute-start(bf16[256,512]{1,0:T(8,128)(2,1)S(1)} %collective-permute-done.3), channel_id=1, source_target_pairs={{0,2},{2,4},{4,6},{6,8},{8,10},{10,12},{12,14},{14,0},{1,3},{3,5},... | collective-permute-start | bytes 786440 | tf_op jit(solution)/shard_map/ppermute | solution.py:65
  253.3 15.7 %collective-permute-start.5 = (bf16[256,512]{1,0:T(8,128)(2,1)S(1)}, bf16[256,512]{1,0:T(8,128)(2,1)S(1)}, u32[]{:S(2)}, u32[]{:S(2)}) collective-permute-start(bf16[256,512]{1,0:T(8,128)(2,1)S(1)} %collective-permute-done.4), channel_id=1, source_target_pairs={{0,2},{2,4},{4,6},{6,8},{8,10},{10,12},{12,14},{14,0},{1,3},{3,5},... | collective-permute-start | bytes 786440 | tf_op jit(solution)/shard_map/ppermute | solution.py:65
  269.0 15.7 %collective-permute-start.6 = (bf16[256,512]{1,0:T(8,128)(2,1)S(1)}, bf16[256,512]{1,0:T(8,128)(2,1)S(1)}, u32[]{:S(2)}, u32[]{:S(2)}) collective-permute-start(bf16[256,512]{1,0:T(8,128)(2,1)S(1)} %collective-permute-done.5), channel_id=1, source_target_pairs={{0,2},{2,4},{4,6},{6,8},{8,10},{10,12},{12,14},{14,0},{1,3},{3,5},... | collective-permute-start | bytes 786440 | tf_op jit(solution)/shard_map/ppermute | solution.py:65
  284.7 17.6 %collective-permute-start.7 = (bf16[256,512]{1,0:T(8,128)(2,1)S(1)}, bf16[256,512]{1,0:T(8,128)(2,1)S(1)}, u32[]{:S(2)}, u32[]{:S(2)}) collective-permute-start(bf16[256,512]{1,0:T(8,128)(2,1)S(1)} %collective-permute-done.6), channel_id=1, source_target_pairs={{0,2},{2,4},{4,6},{6,8},{8,10},{10,12},{12,14},{14,0},{1,3},{3,5},... | collective-permute-start | bytes 786440 | tf_op jit(solution)/shard_map/ppermute | solution.py:65
  305.0 21.6 %collective-permute-start.8 = (bf16[256,4096]{1,0:T(8,128)(2,1)S(1)}, bf16[256,4096]{1,0:T(8,128)(2,1)}, u32[]{:S(2)}, u32[]{:S(2)}) collective-permute-start(bf16[256,4096]{1,0:T(8,128)(2,1)S(1)} %constant_dynamic-slice_fusion), channel_id=1, source_target_pairs={{0,16},{16,0},{1,17},{17,1},{2,18},{18,2},{3,19},{19,3},{4,20},{20... | collective-permute-start | bytes 6291464 | tf_op jit(solution)/shard_map/ppermute | solution.py:70
  306.1 20.3 %collective-permute-start.9 = (bf16[2,512,512]{2,1,0:T(8,128)(2,1)}, bf16[2,512,512]{2,1,0:T(8,128)(2,1)}, u32[]{:S(2)}, u32[]{:S(2)}) collective-permute-start(bf16[2,512,512]{2,1,0:T(8,128)(2,1)} %pad_maximum_fusion.6), channel_id=1, source_target_pairs={{0,1},{17,16},{2,3},{19,18},{4,5},{21,20},{6,7},{23,22},{8,9},{25,... | collective-permute-start | bytes 3145736 | tf_op jit(solution)/shard_map/ppermute | solution.py:56
  317.1 114.8 %collective-permute-start.10 = (bf16[4096,512]{1,0:T(8,128)(2,1)}, bf16[4096,512]{1,0:T(8,128)(2,1)}, u32[]{:S(2)}, u32[]{:S(2)}) collective-permute-start(bf16[4096,512]{1,0:T(8,128)(2,1)} %convert_element_type.57), channel_id=1, source_target_pairs={{0,1},{1,0},{2,3},{3,2},{4,5},{5,4},{6,7},{7,6},{8,9},{9,8},{10,11... | collective-permute-start | bytes 12582920 | tf_op jit(solution)/shard_map/ppermute | solution.py:22
  326.6 13.0 %slice-start = ((s8[8388608]{0:T(1024)(128)(4,1)}), s8[4194304]{0:T(1024)(128)(4,1)S(1)}, s32[]{:S(2)}) async-start(s8[8388608]{0:T(1024)(128)(4,1)} %bitcast.59), calls=%async_computation.6 | async-start | bytes 8388608
  329.8 19.7 %copy-start.2 = (bf16[256,4096]{1,0:T(8,128)(2,1)}, bf16[256,4096]{1,0:T(8,128)(2,1)S(1)}, u32[]{:S(2)}) copy-start(bf16[256,4096]{1,0:T(8,128)(2,1)S(1)} %get-tuple-element.22) | copy-start | bytes 6291460
  329.8 9.7 %slice-start.1 = ((s8[8388608]{0:T(1024)(128)(4,1)}), s8[4194304]{0:T(1024)(128)(4,1)S(1)}, s32[]{:S(2)}) async-start(s8[8388608]{0:T(1024)(128)(4,1)} %bitcast.59), calls=%async_computation.7 | async-start | bytes 8388608
  335.2 9.4 %slice-start.2 = ((s8[8388608]{0:T(1024)(128)(4,1)}), s8[4194304]{0:T(1024)(128)(4,1)S(1)}, s32[]{:S(2)}) async-start(s8[8388608]{0:T(1024)(128)(4,1)} %bitcast.61), calls=%async_computation.8 | async-start | bytes 8388608
  335.2 9.4 %slice-start.3 = ((s8[8388608]{0:T(1024)(128)(4,1)}), s8[4194304]{0:T(1024)(128)(4,1)S(1)}, s32[]{:S(2)}) async-start(s8[8388608]{0:T(1024)(128)(4,1)} %bitcast.61), calls=%async_computation.9 | async-start | bytes 8388608
  335.2 88.1 %collective-permute-start.11 = (bf16[512,512]{1,0:T(8,128)(2,1)S(1)}, bf16[512,512]{1,0:T(8,128)(2,1)S(1)}, u32[]{:S(2)}, u32[]{:S(2)}) collective-permute-start(bf16[512,512]{1,0:T(8,128)(2,1)S(1)} %get-tuple-element.27), channel_id=1, source_target_pairs={{0,1},{1,0},{2,3},{3,2},{4,5},{5,4},{6,7},{7,6},{8,9},{9,8},{10,11... | collective-permute-start | bytes 1572872 | tf_op jit(solution)/shard_map/ppermute | solution.py:22
  423.5 9.4 %copy-start.25 = (bf16[1024,8192]{1,0:T(8,128)(2,1)S(1)}, bf16[1024,8192]{1,0:T(8,128)(2,1)}, u32[]{:S(2)}) copy-start(bf16[1024,8192]{1,0:T(8,128)(2,1)} %all-gather.7.cloned.1.call-done) | copy-start | bytes 50331652
  431.8 7.6 %copy-start.13 = (bf16[512,1024]{1,0:T(8,128)(2,1)S(1)}, bf16[512,1024]{1,0:T(8,128)(2,1)}, u32[]{:S(2)}) copy-start(bf16[512,1024]{1,0:T(8,128)(2,1)} %get-tuple-element.18) | copy-start | bytes 3145732
  444.8 217.3 %collective-permute-start.13 = (bf16[1024,512]{1,0:T(8,128)(2,1)}, bf16[1024,512]{1,0:T(8,128)(2,1)}, u32[]{:S(2)}, u32[]{:S(2)}) collective-permute-start(bf16[1024,512]{1,0:T(8,128)(2,1)} %get-tuple-element.33), channel_id=1, source_target_pairs={{0,1},{1,0},{2,3},{3,2},{4,5},{5,4},{6,7},{7,6},{8,9},{9,8},{10,11... | collective-permute-start | bytes 3145736 | tf_op jit(solution)/shard_map/ppermute | solution.py:22
  447.2 9.6 %copy-start.24 = (bf16[1024,8192]{1,0:T(8,128)(2,1)S(1)}, bf16[1024,8192]{1,0:T(8,128)(2,1)}, u32[]{:S(2)}) copy-start(bf16[1024,8192]{1,0:T(8,128)(2,1)} %all-gather.9.cloned.1.call-done) | copy-start | bytes 50331652
  468.5 195.0 %collective-permute-start.14 = (bf16[1024,512]{1,0:T(8,128)(2,1)}, bf16[1024,512]{1,0:T(8,128)(2,1)}, u32[]{:S(2)}, u32[]{:S(2)}) collective-permute-start(bf16[1024,512]{1,0:T(8,128)(2,1)} %get-tuple-element.31), channel_id=1, source_target_pairs={{0,1},{1,0},{2,3},{3,2},{4,5},{5,4},{6,7},{7,6},{8,9},{9,8},{10,11... | collective-permute-start | bytes 3145736 | tf_op jit(solution)/shard_map/ppermute | solution.py:22
  470.5 10.2 %copy-start.23 = (bf16[1024,8192]{1,0:T(8,128)(2,1)S(1)}, bf16[1024,8192]{1,0:T(8,128)(2,1)}, u32[]{:S(2)}) copy-start(bf16[1024,8192]{1,0:T(8,128)(2,1)} %all-gather.11.cloned.1.call-done) | copy-start | bytes 50331652
  487.4 9.6 %copy-start.11 = (bf16[512,1024]{1,0:T(8,128)(2,1)S(1)}, bf16[512,1024]{1,0:T(8,128)(2,1)}, u32[]{:S(2)}) copy-start(bf16[512,1024]{1,0:T(8,128)(2,1)} %get-tuple-element.19) | copy-start | bytes 3145732
  492.7 172.1 %collective-permute-start.15 = (bf16[1024,512]{1,0:T(8,128)(2,1)}, bf16[1024,512]{1,0:T(8,128)(2,1)}, u32[]{:S(2)}, u32[]{:S(2)}) collective-permute-start(bf16[1024,512]{1,0:T(8,128)(2,1)} %get-tuple-element.29), channel_id=1, source_target_pairs={{0,1},{1,0},{2,3},{3,2},{4,5},{5,4},{6,7},{7,6},{8,9},{9,8},{10,11... | collective-permute-start | bytes 3145736 | tf_op jit(solution)/shard_map/ppermute | solution.py:22
  601.0 9.4 %copy-start.26 = (bf16[1024,8192]{1,0:T(8,128)(2,1)S(1)}, bf16[1024,8192]{1,0:T(8,128)(2,1)}, u32[]{:S(2)}) copy-start(bf16[1024,8192]{1,0:T(8,128)(2,1)} %all-gather.5.cloned.1.call-done) | copy-start | bytes 50331652
  620.6 54.1 %copy-start.7 = (f32[1024,512]{1,0:T(8,128)}, f32[1024,512]{1,0:T(8,128)S(1)}, u32[]{:S(2)}) copy-start(f32[1024,512]{1,0:T(8,128)S(1)} %get-tuple-element.36) | copy-start | bytes 6291460
  620.6 41.4 %collective-permute-start.12 = (bf16[1024,512]{1,0:T(8,128)(2,1)S(1)}, bf16[1024,512]{1,0:T(8,128)(2,1)S(1)}, u32[]{:S(2)}, u32[]{:S(2)}) collective-permute-start(bf16[1024,512]{1,0:T(8,128)(2,1)S(1)} %get-tuple-element.35), channel_id=1, source_target_pairs={{0,1},{1,0},{2,3},{3,2},{4,5},{5,4},{6,7},{7,6},{8,9},{9,8},{10,11... | collective-permute-start | bytes 3145736 | tf_op jit(solution)/shard_map/ppermute | solution.py:22
  622.9 38.9 %collective-permute-start.16 = (bf16[512,512]{1,0:T(8,128)(2,1)S(1)}, bf16[512,512]{1,0:T(8,128)(2,1)S(1)}, u32[]{:S(2)}, u32[]{:S(2)}) collective-permute-start(bf16[512,512]{1,0:T(8,128)(2,1)S(1)} %get-tuple-element.37), channel_id=1, source_target_pairs={{0,1},{1,0},{2,3},{3,2},{4,5},{5,4},{6,7},{7,6},{8,9},{9,8},{10,11... | collective-permute-start | bytes 1572872 | tf_op jit(solution)/shard_map/ppermute | solution.py:22
  666.0 11.7 %copy-start.22 = (bf16[4096,512]{1,0:T(8,128)(2,1)}, bf16[4096,512]{1,0:T(8,128)(2,1)S(1)}, u32[]{:S(2)}) copy-start(bf16[4096,512]{1,0:T(8,128)(2,1)S(1)} %constant_dynamic-update-slice_fusion.16) | copy-start | bytes 12582916
  677.8 7.1 copy-start.15
  689.1 8.3 %copy-start.5 = (f32[1024,512]{1,0:T(8,128)S(1)}, f32[1024,512]{1,0:T(8,128)}, u32[]{:S(2)}) copy-start(f32[1024,512]{1,0:T(8,128)} %get-tuple-element.32) | copy-start | bytes 6291460
  689.1 8.3 %copy-start.12 = (bf16[512,1024]{1,0:T(8,128)(2,1)S(1)}, bf16[512,1024]{1,0:T(8,128)(2,1)}, u32[]{:S(2)}) copy-start(bf16[512,1024]{1,0:T(8,128)(2,1)} %get-tuple-element.19) | copy-start | bytes 3145732
  689.1 8.3 %copy-start.18 = (f32[1024,512]{1,0:T(8,128)S(1)}, f32[1024,512]{1,0:T(8,128)}, u32[]{:S(2)}) copy-start(f32[1024,512]{1,0:T(8,128)} %fusion.15) | copy-start | bytes 6291460
  701.1 8.3 %copy-start.6 = (f32[1024,512]{1,0:T(8,128)S(1)}, f32[1024,512]{1,0:T(8,128)}, u32[]{:S(2)}) copy-start(f32[1024,512]{1,0:T(8,128)} %get-tuple-element.30) | copy-start | bytes 6291460
  701.1 8.3 %copy-start.9 = (bf16[512,1024]{1,0:T(8,128)(2,1)S(1)}, bf16[512,1024]{1,0:T(8,128)(2,1)}, u32[]{:S(2)}) copy-start(bf16[512,1024]{1,0:T(8,128)(2,1)} %get-tuple-element.20) | copy-start | bytes 3145732
  701.2 8.3 %copy-start.17 = (f32[1024,512]{1,0:T(8,128)S(1)}, f32[1024,512]{1,0:T(8,128)}, u32[]{:S(2)}) copy-start(f32[1024,512]{1,0:T(8,128)} %fusion.7) | copy-start | bytes 6291460
  715.7 1.1 collective-permute-start.17
  716.9 3.5 collective-permute-start.18
  720.5 3.5 collective-permute-start.19
  724.1 3.5 collective-permute-start.20
  727.6 4.4 collective-permute-start.21
  734.0 14.1 %copy-start.1 = (bf16[1,512,1024]{2,1,0:T(8,128)(2,1)S(1)}, bf16[1,512,1024]{2,1,0:T(8,128)(2,1)}, u32[]{:S(2)}) copy-start(bf16[1,512,1024]{2,1,0:T(8,128)(2,1)} %param.6) | copy-start | bytes 3145732
  (10 other events, 52.3 us)
Sparse Core Ops, SparseCore 0:
  18.8 168.0 reduce-scatter.1
Sparse Core Ops, SparseCore 1:
  24.8 147.7 all-gather.6
  174.7 163.5 all-gather.8
  340.4 130.0 all-gather.10
  472.8 128.1 all-gather.4
